TPU v7x, 128 devices: a whole 4x4x4 slice. The times are simulated.
128 devices in a mesh: win: 64 (over x, z, y_hi, core), cfg: 2 (over y_lo).
Axes of the slice: x: 4, y: 4 (y_hi: 2, y_lo: 2; y = y_hi * 2 + y_lo), z: 4, core: 2. Of those that a mesh axis runs over, the one named last changes fastest.
Arguments:
- hidden: bfloat16 [2, 65536, 1536], P('cfg', 'win'), may hold values from -36 to 36
- ln_gain: float32 [1536], replicated, may hold values from 0.1 to 1.9
- qkv_weight: bfloat16 [1536, 2304], P('win'), may hold values from -1 to 1
- out_weight: bfloat16 [1536, 768], P('win'), may hold values from -0.4375 to 0.4375
- proj_weight: bfloat16 [1536, 64], replicated, may hold values from -0.15625 to 0.15625
- latent: float32 [32768, 64], P('win'), may hold values from -6 to 6
- conv_in_weight: bfloat16 [7, 64, 1024], replicated, may hold values from -0.25 to 0.25
- snake_in: float32 [1024], replicated, may hold values from 0.5 to 2
- up_weight: bfloat16 [2, 1024, 8, 512], P(None, None, None, 'cfg'), may hold values from -0.125 to 0.125
- snake_mid: float32 [512], replicated, may hold values from 0.5 to 2
- res_weight: bfloat16 [7, 512, 512], replicated, may hold values from -0.09375 to 0.09375
- snake_out: float32 [512], replicated, may hold values from 0.5 to 2
- mix_weight: bfloat16 [512, 512], replicated, may hold values from -0.25 to 0.25
Outputs:
- latent_next: float32 [32768, 64], P('win')
- decoded: bfloat16 [262144, 512], P(('win', 'cfg'))
All inputs are finite; a program needn't handle non-finite values.
Results may differ from a plain program's by a relative error of at most 0.025.
Values may be sent and summed in bfloat16 or wider, within the bound.
A program may use at most 128 MiB of HBM per device.

v0:
```python
import math

import jax
import jax.numpy as jnp
from jax import lax
from jax.sharding import PartitionSpec as P

NH = 12
HS = 64
LAT = 64
OVL = 512
C0 = 1024
C1 = 512
UP = 8
KIN = 7
KRES = 7
HOP = 512


guide_scale = 5.0
euler_step = -0.1
norm_eps = 1e-05


def from_behind(shard, axis, by):
    length = lax.axis_size(axis)
    return lax.ppermute(shard, axis, [(i, (i + by) % length) for i in range(length)])


def with_halo(block, sides, width):
    for axis, dim in sides:
        count = lax.axis_size(axis)
        forward = [(i, i + 1) for i in range(count - 1)]
        forward.append((count - 1, 0))
        backward = [(target, source) for source, target in forward]
        low = lax.ppermute(
            lax.slice_in_dim(block, block.shape[dim] - width, None, axis=dim), axis, forward
        )
        high = lax.ppermute(lax.slice_in_dim(block, 0, width, axis=dim), axis, backward)
        block = jnp.concatenate([low, block, high], axis=dim)
    return block


def layer_norm(widened, ln_gain):
    average = jnp.mean(widened, axis=-1, keepdims=True)
    centred = widened - average
    spread = jnp.mean(centred * centred, axis=-1, keepdims=True)
    return centred * lax.rsqrt(spread + norm_eps) * ln_gain


def snake(inputs, rates):
    return inputs + jnp.sin(rates * inputs) ** 2 / rates


def window_attention(projected):
    head_width = NH * HS
    length = projected.shape[0]
    queries = projected[:, :head_width].reshape(length, NH, HS)
    key_rows = projected[:, head_width : 2 * head_width].reshape(length, NH, HS)
    values = projected[:, 2 * head_width :].reshape(length, NH, HS)
    block_rows = 512
    grouped = queries.reshape(length // block_rows, block_rows, NH, HS)

    def attend_group(query_block):
        scores = jnp.einsum(
            "qhd,khd->hqk", query_block, key_rows, preferred_element_type=jnp.float32
        ) * (1.0 / math.sqrt(HS))
        weights = jax.nn.softmax(scores, axis=-1).astype(jnp.bfloat16)
        attended = jnp.einsum("hqk,khd->qhd", weights, values, preferred_element_type=jnp.float32)
        return attended.astype(jnp.bfloat16)

    attended = lax.map(attend_group, grouped)
    return attended.reshape(length, head_width)


def per_device(
    hidden,
    ln_gain,
    qkv_weight,
    out_weight,
    proj_weight,
    latent,
    conv_in_weight,
    snake_in,
    up_weight,
    snake_mid,
    res_weight,
    snake_out,
    mix_weight,
):
    widened = hidden[0].astype(jnp.float32)
    normed = layer_norm(widened, ln_gain).astype(jnp.bfloat16)
    pair_index = lax.axis_index("cfg")
    projected = jnp.dot(
        normed,
        lax.all_gather(qkv_weight, "win", axis=0, tiled=True),
        preferred_element_type=jnp.float32,
    ).astype(jnp.bfloat16)
    attended = window_attention(projected)
    branch = lax.dot_general(
        attended,
        lax.all_gather(out_weight, "win", axis=0, tiled=True),
        (((1,), (1,)), ((), ())),
        preferred_element_type=jnp.float32,
    )
    residual = (widened + branch).astype(jnp.bfloat16)
    predicted = jnp.dot(residual, proj_weight, preferred_element_type=jnp.float32)
    factor = jnp.where(pair_index == 0, guide_scale, 1.0 - guide_scale)
    offsets = jnp.arange(HOP, dtype=jnp.float32)
    rising = jnp.where(offsets < OVL, (offsets + 0.5) / OVL, 1.0)[:, None]
    falling = 1.0 - rising
    guided = lax.psum((factor * predicted).astype(jnp.bfloat16), "cfg").astype(jnp.float32)
    carried = from_behind(guided[HOP:].astype(jnp.bfloat16), "win", 1).astype(jnp.float32)
    blended = rising * guided[:HOP] + falling * carried
    latent_next = latent + euler_step * blended
    coarse = latent_next.astype(jnp.bfloat16)
    border_width = KIN // 2 + 1
    bordered = with_halo(coarse, (("win", 0),), border_width)
    pair_size = lax.axis_size("cfg")
    half_frames = HOP // pair_size
    flat_in = conv_in_weight.reshape(KIN * LAT, C0)
    local_rows = lax.dynamic_slice_in_dim(
        bordered, pair_index * half_frames, half_frames + 2 * border_width, 0
    )
    tap_stack = jnp.concatenate(
        [local_rows[offset : offset + half_frames + 2] for offset in range(KIN)], axis=1
    )
    start_feat = jnp.dot(tap_stack, flat_in, preferred_element_type=jnp.float32)
    lifted = snake(start_feat, snake_in).astype(jnp.bfloat16)
    current = lifted[1:]
    earlier = lifted[:-1]
    segment = lax.all_gather(up_weight, "cfg", axis=3, tiled=True)
    channels = segment.shape[3]
    blocks = jnp.dot(
        current, segment[0].reshape(C0, UP * channels), preferred_element_type=jnp.float32
    )
    blocks = blocks + jnp.dot(
        earlier, segment[1].reshape(C0, UP * channels), preferred_element_type=jnp.float32
    )
    upsampled = blocks.reshape(current.shape[0], UP, channels)
    flattened = upsampled.reshape((half_frames + 1) * UP, C1)
    res_reach = KRES // 2
    low_edge = UP // 2 - res_reach
    stretched = flattened[low_edge : low_edge + UP * half_frames + 2 * res_reach]
    activated = snake(stretched, snake_mid).astype(jnp.bfloat16)
    convolved = jnp.zeros((UP * half_frames, C1), jnp.float32)
    for tap_index in range(KRES):
        convolved = convolved + jnp.dot(
            activated[tap_index : tap_index + UP * half_frames],
            res_weight[tap_index],
            preferred_element_type=jnp.float32,
        )
    second = snake(convolved, snake_out).astype(jnp.bfloat16)
    centre = stretched[res_reach : res_reach + UP * half_frames]
    decoded = (centre + jnp.dot(second, mix_weight, preferred_element_type=jnp.float32)).astype(
        jnp.bfloat16
    )
    return (latent_next, decoded)


def solution(mesh):
    in_specs = (
        P("cfg", "win", None),
        P(),
        P("win", None),
        P("win", None),
        P(),
        P("win", None),
        P(),
        P(),
        P(None, None, None, "cfg"),
        P(),
        P(),
        P(),
        P(),
    )
    out_specs = (P("win", None), P(("win", "cfg"), None))
    return jax.shard_map(
        per_device, mesh=mesh, in_specs=in_specs, out_specs=out_specs, check_vma=False
    )
```

profile of v0, /device:TPU:1, one launch (start us, length us, event | category | flops | bytes accessed | tf_op | source)
XLA Modules:
  0.0 527.5 jit_solution(4733505800194884858)
XLA Ops:
  7.2 0.0 copy-start
  7.2 0.0 all-gather.4.cloned.1.call-start
  7.2 0.7 all-gather.4.cloned.1.call-update
  7.9 0.0 all-gather.6.cloned.1.call-start
  8.0 0.7 all-gather.6.cloned.1.call-update
  8.7 0.0 all-reduce.2.cloned.1.call-start
  8.7 2.5 convert_reduce_fusion
  11.3 0.3 copy-done.2
  11.6 1.0 fusion.31
  12.6 80.4 %all-gather.4.cloned.1.call-done = bf16[1536,2304]{1,0:T(8,128)(2,1)} async-done(((bf16[24,2304]{1,0:T(8,128)(2,1)}), bf16[1536,2304]{1,0:T(8,128)(2,1)}) %all-gather.4.cloned.1.call-update) | async-done | bytes 7077904 | tf_op jit(solution)/shard_map/all_gather | solution.py:96
  93.0 11.6 %convolution_convert_fusion = bf16[1024,2304]{1,0:T(8,128)(2,1)S(1)} fusion(bf16[1536,2304]{1,0:T(8,128)(2,1)} %all-gather.4.cloned.1.call-done, bf16[1,1024,1536]{2,1,0:T(8,128)(2,1)} %param.15, f32[1536]{0:T(1024)S(1)} %copy-done.10, f32[1024]{0:T(1024)S(1)} %add_rsqrt_fusion, f32[1024]{0:T(1024)S(1)} %broadcast_multiply_fusion), kind=kOutput, calls=%fused_computation.29 | convolution fusion | flops 7257980928 | bytes 14956544 | tf_op jit(solution)/shard_map/dot_general | solution.py:94
  104.6 2.0 fusion.88
  106.5 2.6 copy.18
  109.1 3.8 reshape_reshape.6
  113.0 2.9 copy.21
  115.9 2.6 copy.19
  118.5 1.6 copy.20
  120.1 50.4 %while.10 = (s32[]{:T(128)}, bf16[2,512,12,64]{1,3,2,0:T(8,128)(2,1)}, bf16[2,512,12,64]{1,3,2,0:T(8,128)(2,1)}, bf16[1024,12,64]{0,2,1:T(8,128)(2,1)}, bf16[1024,12,64]{0,2,1:T(8,128)(2,1)}, /*index=5*/s32[]{:T(128)}) while((s32[]{:T(128)}, bf16[2,512,12,64]{1,3,2,0:T(8,128)(2,1)}, bf16[2,512,12,64]{1,3,2,0:T(8,128)(2,1)}, ...), condition=%wide.region_5.6_spmd, body=%wide.region_2.5_spmd.sunk | while | flops 1642464256 | bytes 67690632 | solution.py:72
  120.1 13.2 %fusion.110 = (f32[12,512]{1,0:T(8,128)S(1)}, f32[12,512,1024]{2,1,0:T(8,128)}) fusion(bf16[1024,12,64]{0,2,1:T(8,128)(2,1)} %get-tuple-element.113, bf16[2,512,12,64]{1,3,2,0:T(8,128)(2,1)} %get-tuple-element.112, s32[]{:T(128)S(6)} %copy.29), kind=kOutput, calls=%fused_computation.93.clone.1 | convolution fusion | flops 824181760 | bytes 27549700 | tf_op jit(solution)/shard_map/while/body/eval_jaxpr/sub | solution.py:68
  133.3 10.7 %fusion.111 = bf16[2,512,12,64]{1,3,2,0:T(8,128)(2,1)S(1)} fusion(bf16[2,512,12,64]{1,3,2,0:T(8,128)(2,1)S(1)} %copy-done.3, s32[]{:T(128)S(6)} %copy.29, bf16[1024,12,64]{0,2,1:T(8,128)(2,1)} %get-tuple-element.114, f32[12,512,1024]{2,1,0:T(8,128)} %get-tuple-element.96, f32[12,512]{1,0:T(8,128)S(1)} %get-tuple-element.97), kind=kOutput, calls=%fused_computation.10.clone.1 | convolution fusion | flops 818282496 | bytes 27557892 | tf_op jit(solution)/shard_map/while/body/eval_jaxpr/hqk,khd->qhd/dot_general | solution.py:69
  144.0 1.1 copy-done.4
  145.2 13.3 %fusion.110 = (f32[12,512]{1,0:T(8,128)S(1)}, f32[12,512,1024]{2,1,0:T(8,128)}) fusion(bf16[1024,12,64]{0,2,1:T(8,128)(2,1)} %get-tuple-element.113, bf16[2,512,12,64]{1,3,2,0:T(8,128)(2,1)} %get-tuple-element.112, s32[]{:T(128)S(6)} %copy.29), kind=kOutput, calls=%fused_computation.93.clone.1 | convolution fusion | flops 824181760 | bytes 27549700 | tf_op jit(solution)/shard_map/while/body/eval_jaxpr/sub | solution.py:68
  158.4 10.8 %fusion.111 = bf16[2,512,12,64]{1,3,2,0:T(8,128)(2,1)S(1)} fusion(bf16[2,512,12,64]{1,3,2,0:T(8,128)(2,1)S(1)} %copy-done.3, s32[]{:T(128)S(6)} %copy.29, bf16[1024,12,64]{0,2,1:T(8,128)(2,1)} %get-tuple-element.114, f32[12,512,1024]{2,1,0:T(8,128)} %get-tuple-element.96, f32[12,512]{1,0:T(8,128)S(1)} %get-tuple-element.97), kind=kOutput, calls=%fused_computation.10.clone.1 | convolution fusion | flops 818282496 | bytes 27557892 | tf_op jit(solution)/shard_map/while/body/eval_jaxpr/hqk,khd->qhd/dot_general | solution.py:69
  169.2 1.1 copy-done.4
  170.5 3.1 copy.22
  173.6 0.4 copy.23
  174.0 0.0 all-gather.6.cloned.1.call-done
  174.0 6.8 %fusion.55 = bf16[1024,64]{0,1:T(8,128)(2,1)} fusion(bf16[1536,64]{0,1:T(8,128)(2,1)S(1)} %copy-done.9, bf16[1,1024,1536]{2,1,0:T(8,128)(2,1)} %param.15, bf16[1024,768]{0,1:T(8,128)(2,1)S(1)} %bitcast.110, bf16[1536,768]{1,0:T(8,128)(2,1)} %all-gather.6.cloned.1.call-done, f32[]{:T(128)S(6)} %select_n.21), kind=kOutput, calls=%fused_computation.53 | convolution fusion | flops 2622095360 | bytes 7405572 | tf_op jit(solution)/shard_map/dot_general | solution.py:107
  180.8 0.0 all-reduce.2.cloned.1.call-update
  180.9 0.0 all-gather.8.cloned.1.call-start
  180.9 0.5 all-gather.8.cloned.1.call-update
  181.5 24.5 %all-reduce.2.cloned.1.call-done = bf16[1024,64]{0,1:T(8,128)(2,1)} async-done(((bf16[1024,64]{0,1:T(8,128)(2,1)}), bf16[1024,64]{0,1:T(8,128)(2,1)}) %all-reduce.2.cloned.1.call-update) | async-done | bytes 131088 | tf_op jit(solution)/shard_map/psum | solution.py:112
  206.0 0.8 slice.146
  206.9 3.4 collective-permute-start
  210.3 1.3 collective-permute-done
  211.6 1.5 fusion.81
  213.2 0.1 fusion.89
  213.2 3.9 collective-permute-start.1
  217.1 2.0 collective-permute-start.2
  219.1 0.6 collective-permute-done.1
  219.7 2.1 collective-permute-done.2
  221.8 0.1 fusion.78
  221.9 0.1 slice_dynamic-update-slice_fusion.5
  222.0 0.1 slice_dynamic-update-slice_fusion.4
  222.1 0.1 slice_dynamic-update-slice_fusion.3
  222.2 0.1 slice_dynamic-update-slice_fusion.2
  222.3 0.1 slice_dynamic-update-slice_fusion.1
  222.4 0.1 slice_dynamic-update-slice_fusion
  222.5 4.5 add_convert_fusion.2
  227.0 183.3 %all-gather.8.cloned.1.call-done = bf16[2,1024,8,512]{3,2,1,0:T(8,128)(2,1)} async-done(((bf16[2,1024,8,256]{3,2,1,0:T(8,128)(2,1)}), bf16[2,1024,8,512]{3,2,1,0:T(8,128)(2,1)}) %all-gather.8.cloned.1.call-update) | async-done | bytes 16777232 | tf_op jit(solution)/shard_map/all_gather | solution.py:132
  410.3 11.5 %fusion.87 = (bf16[1,1024,8,512]{3,2,1,0:T(8,128)(2,1)}, bf16[1,1024,8,512]{3,2,1,0:T(8,128)(2,1)}) fusion(bf16[2,1024,8,512]{3,2,1,0:T(8,128)(2,1)} %all-gather.8.cloned.1.call-done), kind=kLoop, calls=%fused_computation.94 | loop fusion | bytes 33554432 | tf_op jit(solution)/shard_map/slice | solution.py:138
  421.9 12.2 %copy.24 = bf16[128,8,8,512]{3,1,2,0:T(8,128)(2,1)} copy(bf16[128,8,8,512]{3,2,1,0:T(8,128)(2,1)} %bitcast.105) | data formatting | bytes 16777216
  434.1 12.2 %copy.25 = bf16[128,8,8,512]{3,1,2,0:T(8,128)(2,1)} copy(bf16[128,8,8,512]{3,2,1,0:T(8,128)(2,1)} %bitcast.104) | data formatting | bytes 16777216
  446.3 6.4 %fusion.59 = f32[257,4096]{1,0:T(8,128)S(1)} fusion(bf16[1024,4096]{1,0:T(8,128)(2,1)} %bitcast.106, bf16[258,1024]{1,0:T(8,128)(2,1)S(1)} %add_convert_fusion.2), kind=kOutput, calls=%fused_computation.56 | convolution fusion | flops 2155872256 | bytes 13127680 | tf_op jit(solution)/shard_map/dot_general | solution.py:134
  452.6 4.5 convolution_add_fusion
  457.2 5.3 %reshape_reshape.7 = f32[2056,512]{1,0:T(8,128)} reshape(f32[257,4096]{1,0:T(8,128)} %convolution_add_fusion) | data formatting | bytes 8421376 | tf_op jit(solution)/shard_map/reshape;reshape | solution.py:141
  462.5 15.9 %add_convert_fusion = bf16[2054,512]{1,0:T(8,128)(2,1)S(1)} fusion(f32[2056,512]{1,0:T(8,128)} %reshape_reshape.7, f32[512]{0:T(512)S(1)} %copy-done.7), kind=kLoop, calls=%fused_computation.31 | loop fusion | flops 5258240 | bytes 6311936 | tf_op jit(solution)/shard_map/convert_element_type | solution.py:145
  478.3 3.2 fusion.41
  481.6 3.3 fusion.43
  484.8 3.2 fusion.45
  488.0 3.2 fusion.47
  491.2 3.3 fusion.51
  494.5 3.2 fusion.49
  497.8 23.0 %fusion.35 = bf16[2048,512]{1,0:T(8,128)(2,1)} fusion(f32[2056,512]{1,0:T(8,128)} %reshape_reshape.7, bf16[512,512]{1,0:T(8,128)(2,1)S(1)} %copy-done.8, f32[2048,512]{1,0:T(8,128)} %fusion.41, f32[2048,512]{1,0:T(8,128)} %fusion.43, f32[2048,512]{1,0:T(8,128)} %fusion.45, f32[2048,512]{1,0:T(8,128)} %fusion.47, f32[2048,512]{1,0:T(8,128)} %fusion.51, ...), kind=kOutput, calls=%fused_computation.33 | convolution fusion | flops 2161115136 | bytes 34605056 | tf_op jit(solution)/shard_map/dot_general | solution.py:155
  (31 shorter events, 0.1 us)
Async XLA Ops:
  7.2 215.3 %copy-start = (bf16[7,64,1024]{2,1,0:T(8,128)(2,1)S(1)}, bf16[7,64,1024]{2,1,0:T(8,128)(2,1)}, u32[]{:S(2)}) copy-start(bf16[7,64,1024]{2,1,0:T(8,128)(2,1)} %param.21) | copy-start | bytes 2752516
  7.2 85.8 %copy-start.10 = (f32[1536]{0:T(1024)S(1)}, f32[1536]{0:T(1024)}, u32[]{:S(2)}) copy-start(f32[1536]{0:T(1024)} %param.16) | copy-start | bytes 18436
  7.2 85.8 %all-gather.4.cloned.1.call-start = ((), (), s32[]{:S(2)}) async-start(), calls=%async_computation | async-start | bytes 7188480 | tf_op jit(solution)/shard_map/all_gather | solution.py:96
  7.9 166.1 %all-gather.6.cloned.1.call-start = ((), (), s32[]{:S(2)}) async-start(), calls=%async_computation.1 | async-start | bytes 2396160 | tf_op jit(solution)/shard_map/all_gather | solution.py:102
  8.7 197.3 %all-reduce.2.cloned.1.call-start = ((), (), s32[]{:S(2)}) async-start(), calls=%async_computation.2 | async-start | bytes 262144 | tf_op jit(solution)/shard_map/psum | solution.py:112
  8.7 2.8 copy-start.2
  120.1 13.2 %copy-start.3 = (bf16[2,512,12,64]{1,3,2,0:T(8,128)(2,1)S(1)}, bf16[2,512,12,64]{1,3,2,0:T(8,128)(2,1)}, u32[]{:S(2)}) copy-start(bf16[2,512,12,64]{1,3,2,0:T(8,128)(2,1)} %get-tuple-element.105) | copy-start | bytes 4718596 | tf_op jit(solution)/shard_map/while
  144.0 1.1 copy-start.4
  145.2 13.3 %copy-start.3 = (bf16[2,512,12,64]{1,3,2,0:T(8,128)(2,1)S(1)}, bf16[2,512,12,64]{1,3,2,0:T(8,128)(2,1)}, u32[]{:S(2)}) copy-start(bf16[2,512,12,64]{1,3,2,0:T(8,128)(2,1)} %get-tuple-element.105) | copy-start | bytes 4718596 | tf_op jit(solution)/shard_map/while
  169.2 1.1 copy-start.4
  170.5 3.5 copy-start.9
  180.9 30.8 %copy-start.5 = (f32[512,64]{0,1:T(8,128)S(1)}, f32[512,64]{0,1:T(8,128)}, u32[]{:S(2)}) copy-start(f32[512,64]{0,1:T(8,128)} %param.20) | copy-start | bytes 393220
  180.9 41.6 %copy-start.11 = (f32[1024]{0:T(1024)S(1)}, f32[1024]{0:T(1024)}, u32[]{:S(2)}) copy-start(f32[1024]{0:T(1024)} %param.22) | copy-start | bytes 12292
  180.9 229.4 %all-gather.8.cloned.1.call-start = ((), (), s32[]{:S(2)}) async-start(), calls=%async_computation.3 | async-start | bytes 25165824 | tf_op jit(solution)/shard_map/all_gather | solution.py:132
  206.9 4.8 collective-permute-start
  213.2 6.5 %collective-permute-start.1 = (bf16[4,64]{0,1:T(8,128)(2,1)S(1)}, bf16[4,64]{0,1:T(8,128)(2,1)S(1)}, u32[]{:S(2)}, u32[]{:S(2)}) collective-permute-start(bf16[4,64]{0,1:T(8,128)(2,1)S(1)} %get-tuple-element.60), channel_id=1, source_target_pairs={{0,2},{2,4},{4,6},{6,8},{8,10},{10,12},{12,14},{14,16},{16,18},{18... | collective-permute-start | bytes 1544 | tf_op jit(solution)/shard_map/ppermute | solution.py:36
  217.1 4.7 collective-permute-start.2
  446.3 6.4 %copy-start.1 = (bf16[128,8,8,512]{3,1,2,0:T(8,128)(2,1)S(1)}, bf16[128,8,8,512]{3,1,2,0:T(8,128)(2,1)}, u32[]{:S(2)}) copy-start(bf16[128,8,8,512]{3,1,2,0:T(8,128)(2,1)} %copy.25) | copy-start | bytes 25165828
  457.2 5.3 %copy-start.7 = (f32[512]{0:T(512)S(1)}, f32[512]{0:T(512)}, u32[]{:S(2)}) copy-start(f32[512]{0:T(512)} %param.24) | copy-start | bytes 6148
  462.5 15.9 %copy-start.6 = (bf16[7,512,512]{2,1,0:T(8,128)(2,1)S(1)}, bf16[7,512,512]{2,1,0:T(8,128)(2,1)}, u32[]{:S(2)}) copy-start(bf16[7,512,512]{2,1,0:T(8,128)(2,1)} %param.25) | copy-start | bytes 11010052
  494.5 3.3 copy-start.8
  494.5 3.3 copy-start.12
Sparse Core Ops, SparseCore 0:
  11.3 81.6 all-gather.3
  96.2 66.0 all-gather.5
  181.0 24.9 all-reduce.1
  207.5 202.7 all-gather.7
where the time goes:
time: 536 us; the launch traced here: 527 us
  waiting for transfers between devices  294 us (55%)
  matrix products  124 us (23%)
  local copies, waits for them, and re-layouts  64.3 us (12%)
  other arithmetic  21 us (4%)
  between operations  14.2 us (3%)
  starting transfers between devices  9.46 us (2%)
    all_gather x1, waiting for transfers between devices, per_device(): segment = lax.all_gather(up_weight, 'cfg', axis=3, tiled=True)  183 us
    all_gather x1, waiting for transfers between devices, per_device(): lax.all_gather(qkv_weight, 'win', axis=0, tiled=True)  80.4 us
    sub x2, matrix products, attend_group(): weights = jax.nn.softmax(scores, axis=-1).astype(jnp.bfloat16)  26.4 us
    unnamed x31, local copies, waits for them, and re-layouts  25.6 us
    psum x1, waiting for transfers between devices, per_device(): lax.psum((factor * predicted).astype(jnp.bfloat16), 'cfg')  24.5 us
    dot_general x1, matrix products, per_device(): jnp.dot(second, mix_weight, preferred_element_type=jnp.float32)  23 us
    dot_general x2, matrix products, attend_group(): jnp.einsum('hqk,khd->qhd', weights, values, preferred_element_type=jnp.fl...  21.5 us
    dot_general x6, matrix products, per_device(): jnp.dot(activated[tap_index:tap_index + UP * half_frames], res_weight[tap...  19.4 us
  transfers between devices with their start and end apart: 7, of which 6 were waited for; matrix products, arithmetic and copies ran while one was open for 17% of the time, Pallas kernels for 0%

commit v1 on v0

v1 whole, which is shorter than its diff:
```python
import math
import jax
import jax.numpy as jnp
from jax import lax
from jax.sharding import PartitionSpec as P
from jax.experimental import pallas as pl
from jax.experimental.pallas import tpu as pltpu

F32 = jnp.float32
BF16 = jnp.bfloat16
SIN_COEF = (9.869524955749512, -32.46514129638672, 42.64342498779297, -29.426273345947266, 10.581298828125)

guide_scale = 5.0
euler_step = -0.1
norm_eps = 1e-05


MESH = pl.DeviceIdType.MESH
CHUNKS = 4


def front_kernel(hid_hbm, gain_ref, qkv_ref, wo_ref, proj_ref, lat_ref, up_hbm,
                 own_out, part_out, prev_out, nxt_out, pp_out, lat_out, u_own, u_oth,
                 hid, normed, first, arrived0, wbuf, qkv, attended, pred, xs, edge, uin, urel,
                 load_sem, s0, r0, gs, gr, ls, lr, us, ur, xsend, xrecv, own_sem):
    win, cfg = lax.axis_index("win"), lax.axis_index("cfg")
    core, hi, z, x = lax.rem(win, 2), lax.rem(win // 2, 2), lax.rem(win // 4, 4), win // 16
    n_win = lax.axis_size("win")

    def at(x, z, hi, core):
        return ((x * 4 + z) * 2 + hi) * 2 + core

    other = 1 - cfg
    sibling = (at(x, z, hi, 1 - core), cfg)
    x_up, x_dn = lax.rem(x + 1, 4), lax.rem(x + 3, 4)
    z_up, z_dn = lax.rem(z + 1, 4), lax.rem(z + 3, 4)
    across = [(at(x, z, 1 - hi, 0), other), (at(x, z, 1 - hi, 1), other)]
    facing = (win, other)
    opposite = (at(x, z, 1 - hi, core), other)
    right, left = lax.rem(win + 1, n_win), lax.rem(win + n_win - 1, n_win)
    right2, left2 = lax.rem(win + 2, n_win), lax.rem(win + n_win - 2, n_win)
    to_x_up, to_x_dn = (at(x_up, z, hi, core), cfg), (at(x_dn, z, hi, core), cfg)
    to_z_up, to_z_dn = (at(x, z_up, hi, core), cfg), (at(x, z_dn, hi, core), cfg)

    def remote(src, dst, ssem, rsem, device):
        return pltpu.make_async_remote_copy(src_ref=src, dst_ref=dst, send_sem=ssem, recv_sem=rsem,
                                            device_id=device, device_id_type=MESH)

    def await_in(dst, ssem, rsem):
        remote(dst, dst, ssem, rsem, sibling).wait_recv()

    hid_copy = pltpu.make_async_copy(hid_hbm, hid, load_sem.at[0])
    hid_copy.start()
    uin_copy = pltpu.make_async_copy(up_hbm.at[core], uin, load_sem.at[1])
    uin_copy.start()

    barrier = pltpu.get_barrier_semaphore()
    partners = [sibling, across[0], across[1], to_x_up, to_x_dn, to_z_up, to_z_dn, facing]
    partners += [(w, c) for w in (right, left, right2, left2) for c in (cfg, other)]
    for p in partners:
        pl.semaphore_signal(barrier, inc=1, device_id=p, device_id_type=MESH)

    for c in range(2):
        for i in range(3):
            for part in range(3):
                col = part * 768 + 128 * (2 * i + c)
                first[c, i, 0:24, part * 128:(part + 1) * 128] = qkv_ref[:, col:col + 128]
        first[c, 3, 0:24, :] = wo_ref[:, 384 * c:384 * (c + 1)]
        for i in range(4):
            first[c, i, 24:32, :] = jnp.zeros((8, 384), BF16)
    edge[:, 64:128] = jnp.zeros((32, 64), F32)
    edge[0:16, 0:64] = lat_ref[0:16]
    edge[16:32, 0:64] = lat_ref[496:512]
    pl.semaphore_wait(barrier, len(partners))

    mine = hi * 2 + core
    sends = []

    def go(copy):
        copy.start()
        sends.append(copy)

    go(remote(first.at[1 - core], arrived0.at[mine], s0.at[0], r0.at[mine], sibling))
    for c in range(2):
        go(remote(first.at[c], arrived0.at[mine], s0.at[1 + c], r0.at[mine], across[c]))
    go(remote(edge.at[0:16], lat_out.at[1], ls.at[0], lr.at[1], (left, cfg)))
    go(remote(edge.at[16:32], lat_out.at[0], ls.at[1], lr.at[0], (right, cfg)))

    def views(i):
        a1 = lambda p: wbuf.at[i, core, p, z, 0:48]
        b1 = lambda p: wbuf.at[i, core, x, p, 48:96]
        a2 = lambda r, lo, n: wbuf.at[i, core, pl.ds(lo, n), r, 0:48]
        b2 = lambda r, lo, n: wbuf.at[i, core, r, pl.ds(lo, n), 48:96]
        ring_a = (x, x_up, x_dn, to_x_up, to_x_dn)
        ring_b = (z, z_up, z_dn, to_z_up, to_z_dn)
        return ((a1, a2, ring_a, ring_b, 0), (b1, b2, ring_b, ring_a, 7))

    def stage1(i):
        out = []
        for one, _, (me, up, dn, to_up, to_dn), _, k in views(i):
            out.append(remote(one(me), one(me), gs.at[i, k], gr.at[i, k], to_up))
            out.append(remote(one(me), one(me), gs.at[i, k + 1], gr.at[i, k + 1], to_dn))
        return out

    def stage1_in(i):
        for one, _, (me, up, dn, to_up, to_dn), _, k in views(i):
            await_in(one(dn), gs.at[i, k], gr.at[i, k])
            await_in(one(up), gs.at[i, k + 1], gr.at[i, k + 1])

    def forward1(i):
        return [remote(one(dn), one(dn), gs.at[i, k + 2], gr.at[i, k + 2], to_up)
                for one, _, (me, up, dn, to_up, to_dn), _, k in views(i)]

    def forward1_in(i):
        for one, _, (me, up, dn, to_up, to_dn), _, k in views(i):
            await_in(one(lax.rem(me + 2, 4)), gs.at[i, k + 2], gr.at[i, k + 2])

    def stage2(i):
        out = []
        for _, two, _, (me, up, dn, to_up, to_dn), k in views(i):
            out.append(remote(two(me, 0, 4), two(me, 0, 4), gs.at[i, k + 3], gr.at[i, k + 3], to_up))
            out.append(remote(two(me, 0, 4), two(me, 0, 4), gs.at[i, k + 4], gr.at[i, k + 4], to_dn))
        return out

    def stage2_in(i):
        for _, two, _, (me, up, dn, to_up, to_dn), k in views(i):
            await_in(two(dn, 0, 4), gs.at[i, k + 3], gr.at[i, k + 3])
            await_in(two(up, 0, 4), gs.at[i, k + 4], gr.at[i, k + 4])

    def forward2(i):
        out = []
        for _, two, _, (me, up, dn, to_up, to_dn), k in views(i):
            out.append(remote(two(dn, 0, 2), two(dn, 0, 2), gs.at[i, k + 5], gr.at[i, k + 5], to_up))
            out.append(remote(two(up, 2, 2), two(up, 2, 2), gs.at[i, k + 6], gr.at[i, k + 6], to_dn))
        return out

    def forward2_in(i):
        for _, two, _, (me, up, dn, to_up, to_dn), k in views(i):
            far = lax.rem(me + 2, 4)
            await_in(two(far, 0, 2), gs.at[i, k + 5], gr.at[i, k + 5])
            await_in(two(far, 2, 2), gs.at[i, k + 6], gr.at[i, k + 6])

    def share(i):
        return [remote(wbuf.at[i, core], wbuf.at[i, core], gs.at[i, 14], gr.at[i, 14], sibling)]

    def share_in(i):
        await_in(wbuf.at[i, 1 - core], gs.at[i, 14], gr.at[i, 14])

    def launch(copies):
        for copy in copies:
            copy.start()

    def assemble(i):
        rows = jnp.concatenate([arrived0[p, i].astype(F32)[0:24] for p in range(4)], axis=0)
        wbuf[i, core, x, z] = rows.astype(BF16)

    def norm_rows(b, carry):
        r = pl.ds(pl.multiple_of(b * 128, 128), 128)
        v = hid[r, :].astype(F32)
        centred = v - jnp.mean(v, axis=-1, keepdims=True)
        spread = jnp.mean(centred * centred, axis=-1, keepdims=True)
        normed[r, :] = (centred * lax.rsqrt(spread + norm_eps) * gain_ref[...]).astype(BF16)
        return carry

    def turn_rows(b, carry):
        r = pl.ds(pl.multiple_of(b * 128, 128), 128)
        urel[:, r, :] = jnp.swapaxes(uin[r], 0, 1)
        return carry

    hid_copy.wait()
    lax.fori_loop(0, 4, norm_rows, 0)
    arrived0[mine] = first[core]
    for p in (hi * 2 + 1 - core, (1 - hi) * 2, (1 - hi) * 2 + 1):
        await_in(arrived0.at[p], s0.at[0], r0.at[p])
    assemble(0)
    launch(stage1(0))
    for i in range(1, CHUNKS):
        assemble(i)
    lax.fori_loop(4, 8, norm_rows, 0)
    stage1_in(0)
    launch(forward1(0))
    pred[...] = jnp.dot(hid[...], proj_ref[...], preferred_element_type=F32)
    forward1_in(0)
    launch(stage2(0))
    launch(stage1(1))
    uin_copy.wait()
    lax.fori_loop(0, 4, turn_rows, 0)
    stage2_in(0)
    launch(forward2(0))
    lax.fori_loop(4, 8, turn_rows, 0)

    up_local = pltpu.make_async_copy(urel, u_own.at[:, core], load_sem.at[2])
    up_local.start()
    go(remote(urel, u_own.at[:, core], us.at[0], ur.at[0], sibling))
    go(remote(urel.at[0:4], u_oth.at[0:4, core], us.at[1], ur.at[1], facing))
    go(remote(urel.at[4:8], u_oth.at[4:8, core], us.at[2], ur.at[2], opposite))
    forward2_in(0)
    launch(share(0))
    share_in(0)

    lane_first = lax.broadcasted_iota(jnp.int32, (1, 128), 1) < 64
    one = jnp.ones((), BF16)
    pick = [jnp.where(lane_first, 0.125, 0.0).astype(BF16), jnp.where(lane_first, 0.0, 0.125).astype(BF16)]

    def chunk(i, carry):
        nxt = i + 1
        stage1_in(nxt)
        launch(forward1(nxt))

        def project(b, carry):
            r = pl.ds(pl.multiple_of(b * 256, 256), 256)
            w = jnp.concatenate([wbuf[i, 0].reshape(1536, 384), wbuf[i, 1].reshape(1536, 384)], axis=1)
            res = jnp.dot(normed[r, :], w, preferred_element_type=F32).astype(BF16)
            for g in range(6):
                qkv[g, r, :] = res[:, g * 128:(g + 1) * 128]
            return carry
        lax.fori_loop(0, 4, project, 0)
        forward1_in(nxt)
        launch(stage2(nxt))

        @pl.when(i < 2)
        def _():
            launch(stage1(nxt + 1))

        def heads(c, carry):
            k, v = qkv[3 * c + 1], qkv[3 * c + 2]
            vs = (jnp.where(lane_first, v, one), jnp.where(lane_first, one, v))

            def score(t):
                q = qkv[3 * c, t // 2 * 256:(t // 2 + 1) * 256] * pick[t % 2]
                return lax.dot_general(q, k, (((1,), (1,)), ((), ())), preferred_element_type=F32)
            s, keep = score(0), None
            for t in range(8):
                s_next = score(t + 1) if t < 7 else None
                p = jnp.exp(s - jnp.max(s, axis=-1, keepdims=True)).astype(BF16)
                o = jnp.dot(p, vs[t % 2], preferred_element_type=F32)
                o = o / pltpu.roll(o, 64, 1)
                if t % 2:
                    attended[2 * i + c, t // 2 * 256:(t // 2 + 1) * 256] = jnp.where(lane_first, keep, o).astype(BF16)
                keep, s = o, s_next

            @pl.when(c == 0)
            def _():
                stage2_in(nxt)
                launch(forward2(nxt))
            return carry
        lax.fori_loop(0, 2, heads, 0)
        forward2_in(nxt)
        launch(share(nxt))
        share_in(nxt)
        return carry
    lax.fori_loop(0, 3, chunk, 0)

    factor = jnp.where(cfg == 0, guide_scale, 1.0 - guide_scale).astype(F32)
    wo = jnp.concatenate([wbuf[3, 0].reshape(1536, 384), wbuf[3, 1].reshape(1536, 384)], axis=1)
    folded = lax.dot_general(proj_ref[...], wo, (((0,), (0,)), ((), ())), preferred_element_type=F32).astype(BF16)
    att = jnp.concatenate([attended[g] for g in range(6)], axis=1)
    total = pred[...] + lax.dot_general(att, folded, (((1,), (1,)), ((), ())), preferred_element_type=F32)
    xs[:, 0:64] = (factor * total).astype(BF16)
    xs[:, 64:128] = jnp.zeros((1024, 64), BF16)
    own_copy = pltpu.make_async_copy(xs.at[0:528], own_out, own_sem)
    own_copy.start()
    for c, to in ((0, cfg), (1, other)):
        go(remote(xs.at[496:1024], prev_out.at[cfg], xsend.at[c], xrecv.at[cfg], (right, to)))
        go(remote(xs.at[0:16], nxt_out.at[cfg], xsend.at[2 + c], xrecv.at[2 + cfg], (left, to)))
        go(remote(xs.at[1008:1024], pp_out.at[cfg], xsend.at[4 + c], xrecv.at[4 + cfg], (right2, to)))
    go(remote(xs.at[0:528], part_out, xsend.at[6], xrecv.at[6], facing))

    await_in(u_oth.at[0:4, core], us.at[1], ur.at[1])
    go(remote(u_oth.at[0:4, core], u_oth.at[0:4, core], us.at[3], ur.at[3], sibling))
    await_in(u_oth.at[4:8, core], us.at[2], ur.at[2])
    go(remote(u_oth.at[4:8, core], u_oth.at[4:8, core], us.at[4], ur.at[4], sibling))

    for c in range(2):
        await_in(prev_out.at[c], xsend.at[0], xrecv.at[c])
        await_in(nxt_out.at[c], xsend.at[0], xrecv.at[2 + c])
        await_in(pp_out.at[c], xsend.at[0], xrecv.at[4 + c])
        await_in(lat_out.at[c], ls.at[0], lr.at[c])
    await_in(part_out, xsend.at[6], xrecv.at[6])
    await_in(u_own.at[:, 1 - core], us.at[0], ur.at[0])
    await_in(u_oth.at[0:4, 1 - core], us.at[3], ur.at[3])
    await_in(u_oth.at[4:8, 1 - core], us.at[4], ur.at[4])
    up_local.wait()
    own_copy.wait()
    for copy in sends:
        copy.wait_send()

    def drain(i, carry):
        for copies in (stage1(i), forward1(i), stage2(i), forward2(i), share(i)):
            for copy in copies:
                copy.wait_send()
        return carry
    lax.fori_loop(0, CHUNKS, drain, 0)


def front(hidden, gain, qkv_weight, out_weight, proj_weight, latent, up_weight):
    vm = pl.BlockSpec(memory_space=pltpu.VMEM)
    hbm = pl.BlockSpec(memory_space=pl.ANY)
    dma = pltpu.SemaphoreType.DMA
    shape = jax.ShapeDtypeStruct
    return pl.pallas_call(
        front_kernel,
        out_shape=(shape((528, 128), BF16), shape((528, 128), BF16), shape((2, 528, 128), BF16),
                   shape((2, 16, 128), BF16), shape((2, 16, 128), BF16), shape((2, 16, 128), F32),
                   shape((8, 2, 1024, 256), BF16), shape((8, 2, 1024, 256), BF16)),
        in_specs=[hbm, vm, vm, vm, vm, vm, hbm],
        out_specs=(hbm,) * 8,
        scratch_shapes=[
            pltpu.VMEM((1024, 1536), BF16),
            pltpu.VMEM((1024, 1536), BF16),
            pltpu.VMEM((2, 4, 32, 384), BF16),
            pltpu.VMEM((4, 4, 32, 384), BF16),
            pltpu.VMEM((CHUNKS, 2, 4, 4, 96, 384), BF16),
            pltpu.VMEM((6, 1024, 128), BF16),
            pltpu.VMEM((6, 1024, 128), BF16),
            pltpu.VMEM((1024, 64), F32),
            pltpu.VMEM((1024, 128), BF16),
            pltpu.VMEM((32, 128), F32),
            pltpu.VMEM((1024, 8, 256), BF16),
            pltpu.VMEM((8, 1024, 256), BF16),
            dma((3,)), dma((3,)), dma((4,)), dma((CHUNKS, 15)), dma((CHUNKS, 15)),
            dma((2,)), dma((2,)), dma((5,)), dma((5,)), dma((7,)), dma((7,)), dma,
        ],
        compiler_params=pltpu.CompilerParams(collective_id=0, has_side_effects=True,
                                             vmem_limit_bytes=56 * 1024 * 1024),
        cost_estimate=pl.CostEstimate(flops=14_000_000_000, bytes_accessed=40_000_000, transcendentals=12_600_000),
        name="front",
    )(hidden, gain, qkv_weight, out_weight, proj_weight, latent, up_weight)


def snake(v, scale, inverse):
    t = v * scale
    r = t - jnp.round(t)
    s = r * r
    acc = SIN_COEF[4]
    for c in SIN_COEF[3::-1]:
        acc = acc * s + c
    return v + acc * (s * inverse)


PAD = 16


def decode_kernel(own_ref, part_ref, prev_ref, nxt_ref, pp_ref, halo_ref, lat_ref, cw_ref, a_in_ref, a_mid_ref, a_out_ref,
                  u_own, u_oth, res_hbm, mix_hbm, lat_out, dec_out,
                  ext, lifted, pair, ubuf, act, ups, res, mix, outf, u_sem, w_sem):
    side = lax.axis_index("cfg")
    ucopies = []
    for j in range(8):
        for h, src in ((0, u_own), (1, u_oth)):
            cp = pltpu.make_async_copy(src.at[j], ubuf.at[j, h], u_sem.at[j, h])
            cp.start()
            ucopies.append(cp)
    rcopy = pltpu.make_async_copy(res_hbm, res, w_sem.at[0])
    rcopy.start()
    mcopy = pltpu.make_async_copy(mix_hbm, mix, w_sem.at[1])
    mcopy.start()

    def f32(x):
        return x.astype(F32)
    head = jnp.concatenate([
        f32(prev_ref[0, 0:16]) + f32(prev_ref[1, 0:16]),
        f32(own_ref[0:512]) + f32(part_ref[0:512]),
        f32(nxt_ref[0]) + f32(nxt_ref[1])], axis=0)
    tail = jnp.concatenate([
        f32(pp_ref[0]) + f32(pp_ref[1]),
        f32(prev_ref[0, 16:528]) + f32(prev_ref[1, 16:528]),
        f32(own_ref[512:528]) + f32(part_ref[512:528])], axis=0)
    row = lax.broadcasted_iota(jnp.int32, (544, 128), 0) - PAD
    row = jnp.where(row < 0, row + 512, jnp.where(row >= 512, row - 512, row))
    rising = (row.astype(F32) + 0.5) * (1.0 / 512)
    blended = rising * head + (1.0 - rising) * tail
    extended = jnp.concatenate([halo_ref[0][:, :64], lat_ref[...], halo_ref[1][:, :64]], axis=0)
    nxt_lat = extended + euler_step * blended[:, :64]
    lat_out[...] = nxt_lat[16:528]
    ext[0:544, :] = nxt_lat.astype(BF16).astype(F32)
    ext[544:560, :] = jnp.zeros((16, 64), F32)

    a_in = a_in_ref[...]
    x = ext[pl.ds(pl.multiple_of(side * 256, 256), 296), :]
    acc = None
    for k in range(7):
        d = jnp.dot(x[12 + k:12 + k + 272].astype(BF16), cw_ref[k], preferred_element_type=F32)
        acc = d if acc is None else acc + d
    lifted[...] = snake(acc, a_in * (1 / math.pi), 1.0 / a_in)
    pair[:, 0:1024] = lifted[1:265, :].astype(BF16)
    pair[:, 1024:2048] = lifted[0:264, :].astype(BF16)

    a_mid = a_mid_ref[...]
    mid_scale, mid_inv = a_mid * (1 / math.pi), 1.0 / a_mid
    lhs = pair[...]

    for j in range(8):
        for h in range(2):
            ucopies[2 * j + h].wait()
            cols = pl.multiple_of((side * (1 - 2 * h) + h) * 256, 256)
            outf_blk = jnp.dot(lhs, ubuf[j, h], preferred_element_type=F32)
            lifted[0:264, pl.ds(cols, 256)] = outf_blk
        blk = lifted[0:264, 0:512]
        s = snake(blk, mid_scale, mid_inv)
        if j < 4:
            ups[j + 4] = lifted[1:257, 0:512]
        else:
            ups[j - 4] = blk[0:256]
        act[j] = s[0:256].astype(BF16)
        lifted[0:264, 512:1024] = s
        act[j + 8] = lifted[1:257, 512:1024].astype(BF16)

    rcopy.wait()
    mcopy.wait()
    a_out = a_out_ref[...]
    out_scale, out_inv = a_out * (1 / math.pi), 1.0 / a_out

    def step(i, carry):
        conv = None
        for k in range(7):
            d = jnp.dot(act[i + 1 + k], res[k], preferred_element_type=F32)
            conv = d if conv is None else conv + d
        second = snake(conv, out_scale, out_inv).astype(BF16)
        outf[:, i, :] = ups[i] + jnp.dot(second, mix[...], preferred_element_type=F32)
        return carry
    lax.fori_loop(0, 8, step, 0)
    dec_out[...] = outf[...].reshape(2048, 512).astype(BF16)


def decode_call(own, part, prev, nxt, pp, halo, lat, cw, a_in, a_mid, a_out, u_own, u_oth, res, mix):
    vm = pl.BlockSpec(memory_space=pltpu.VMEM)
    anyspec = pl.BlockSpec(memory_space=pl.ANY)
    return pl.pallas_call(
        decode_kernel,
        out_shape=(jax.ShapeDtypeStruct((512, 64), F32), jax.ShapeDtypeStruct((2048, 512), BF16)),
        in_specs=[vm] * 11 + [anyspec] * 4,
        out_specs=(vm, vm),
        scratch_shapes=[
            pltpu.VMEM((560, 64), F32),
            pltpu.VMEM((272, 1024), F32),
            pltpu.VMEM((264, 2048), BF16),
            pltpu.VMEM((8, 2, 2048, 256), BF16),
            pltpu.VMEM((16, 256, 512), BF16),
            pltpu.VMEM((8, 256, 512), F32),
            pltpu.VMEM((7, 512, 512), BF16),
            pltpu.VMEM((512, 512), BF16),
            pltpu.VMEM((256, 8, 512), F32),
            pltpu.SemaphoreType.DMA((8, 2)),
            pltpu.SemaphoreType.DMA((2,)),
        ],
        compiler_params=pltpu.CompilerParams(vmem_limit_bytes=56 * 1024 * 1024),
        name="decode",
    )(own, part, prev, nxt, pp, halo, lat, cw, a_in, a_mid, a_out, u_own, u_oth, res, mix)


def per_device(hidden, ln_gain, qkv_weight, out_weight, proj_weight, latent, conv_in_weight, snake_in,
               up_weight, snake_mid, res_weight, snake_out, mix_weight):
    own, part, prev, nxt, pp, halo, u_own, u_oth = front(
        hidden[0], ln_gain.reshape(1, -1), qkv_weight, out_weight, proj_weight, latent, up_weight)
    return decode_call(own, part, prev, nxt, pp, halo, latent, conv_in_weight,
                       snake_in.reshape(1, -1), snake_mid.reshape(1, -1), snake_out.reshape(1, -1),
                       u_own.reshape(8, 2048, 256), u_oth.reshape(8, 2048, 256), res_weight, mix_weight)


def solution(mesh):
    in_specs = (
        P("cfg", "win", None),
        P(),
        P("win", None),
        P("win", None),
        P(),
        P("win", None),
        P(),
        P(),
        P(None, None, None, "cfg"),
        P(),
        P(),
        P(),
        P(),
    )
    out_specs = (P("win", None), P(("win", "cfg"), None))
    return jax.shard_map(
        per_device, mesh=mesh, in_specs=in_specs, out_specs=out_specs, check_vma=False
    )
```

time: 536 us -> 132 us (0.25); the launches traced: 527 us -> 132 us
  waiting for transfers between devices: 294 us -> 0 us
  Pallas kernels: 0 us -> 125 us
  matrix products: 124 us -> 0 us
  local copies, waits for them, and re-layouts: 64.3 us -> 6.6 us
  other arithmetic: 21 us -> 0 us
  between operations: 14.2 us -> 0.65 us
  starting transfers between devices: 9.46 us -> 0 us
    all_gather x3 -> x0, waiting for transfers between devices: 264 us -> none  [the longest x1 183 us: per_device(): segment = lax.all_gather(up_weight, 'cfg', axis=3, tiled=True)]
    pallas_call x0 -> x2, Pallas kernels: none -> 125 us  [the longest x1 92.5 us: front(): pl.pallas_call(front_kernel, out_shape=(shape((528, 128), BF16), shape((5...]
    dot_general x14 -> x0, matrix products: 97.7 us -> none  [the longest x1 23 us: per_device(): jnp.dot(second, mix_weight, preferred_element_type=jnp.float32)]
    sub x2 -> x0, matrix products: 26.4 us -> none  [attend_group(): weights = jax.nn.softmax(scores, axis=-1).astype(jnp.bfloat16)]
    psum x1 -> x0, waiting for transfers between devices: 24.5 us -> none  [per_device(): lax.psum((factor * predicted).astype(jnp.bfloat16), 'cfg')]
    unnamed x31 -> x2, local copies, waits for them, and re-layouts: 25.6 us -> 3.59 us
    slice x7 -> x0, local copies, waits for them, and re-layouts: 21.2 us -> none  [the longest x1 11.5 us: per_device(): segment[1].reshape(C0, UP * channels)]
    convert_element_type x2 -> x0, other arithmetic: 17.4 us -> none  [the longest x1 15.9 us: per_device(): activated = snake(stretched, snake_mid).astype(jnp.bfloat16)]
  transfers between devices with their start and end apart: 7 -> 0, of which waited for: 6 -> 0; matrix products, arithmetic and copies ran while one was open for 17% -> 0% of each run, Pallas kernels for 0% -> 0%
where the time goes in v1:
time: 132 us
  Pallas kernels  125 us (95%)
  local copies, waits for them, and re-layouts  6.6 us (5%)
    pallas_call x1, Pallas kernels, front(): pl.pallas_call(front_kernel, out_shape=(shape((528, 128), BF16), shape((5...  92.5 us
    pallas_call x1, Pallas kernels, decode_call(): pl.pallas_call(decode_kernel, out_shape=(jax.ShapeDtypeStruct((512, 64),...  32.2 us
    unnamed x2, local copies, waits for them, and re-layouts  3.59 us

profile of v1, /device:TPU:1, one launch (start us, length us, event | category | flops | bytes accessed | tf_op | source)
XLA Modules:
  0.0 132.0 jit_solution(8951623972038770457)
XLA Ops:
  0.6 1.3 reshape.22.gain_ref
  1.9 1.7 %copy.16.lat_ref = f32[512,64]{1,0:T(8,128)} copy(f32[512,64]{0,1:T(8,128)} %param.18) | data formatting | bytes 262144 | tf_op args[5]
  3.7 1.8 %copy.15.proj_ref = bf16[1536,64]{1,0:T(8,128)(2,1)} copy(bf16[1536,64]{0,1:T(8,128)(2,1)} %param.17) | data formatting | bytes 393216 | tf_op args[4]
  5.5 92.5 %front.1 = (bf16[528,128]{1,0:T(8,128)(2,1)}, bf16[528,128]{1,0:T(8,128)(2,1)}, bf16[2,528,128]{2,1,0:T(8,128)(2,1)}, bf16[2,16,128]{2,1,0:T(8,128)(2,1)}, bf16[...) custom-call(bf16[1024,1536]{1,0:T(8,128)(2,1)} %bitcast.11, ...), custom_call_target="tpu_custom_call" | custom-call | flops 14000000000 | bytes 40000000 | tf_op jit(solution)/shard_map/front/pallas_call | solution.py:301
  98.0 32.2 %decode.1 = (f32[512,64]{1,0:T(8,128)}, bf16[2048,512]{1,0:T(8,128)(2,1)}) custom-call(bf16[528,128]{1,0:T(8,128)(2,1)} %get-tuple-element.10.own_ref, bf16[528,128]{1,0:T(8,128)(2,1)} %get-tuple-element.11.part_ref, bf16[2,528,128]{2,1,0:T(8,128)(2,1)} %get-tuple-element.12.prev_ref, bf16[2,16,128]{2,1,0:T(8,128)(2,1)} %get-tuple-element.13.nxt_ref, ...), custom_call_target="tpu_custom_call" | custom-call | tf_op jit(solution)/shard_map/decode/pallas_call | solution.py:429
  130.2 1.7 %copy.18 = f32[512,64]{0,1:T(8,128)} copy(f32[512,64]{1,0:T(8,128)} %get-tuple-element.18) | data formatting | bytes 262144 | tf_op jit(solution)/shard_map/decode/pallas_call | solution.py:429

commit v2 on v1

--- a/solution.py
+++ b/solution.py
@@ -21,7 +21,7 @@
 
 def front_kernel(hid_hbm, gain_ref, qkv_ref, wo_ref, proj_ref, lat_ref, up_hbm,
                  own_out, part_out, prev_out, nxt_out, pp_out, lat_out, u_own, u_oth,
-                 hid, normed, first, arrived0, wbuf, qkv, attended, pred, xs, edge, uin, urel,
+                 hid, normed, first, arrived0, wbuf, qkv, attended, pred, xs, uin, urel,
                  load_sem, s0, r0, gs, gr, ls, lr, us, ur, xsend, xrecv, own_sem):
     win, cfg = lax.axis_index("win"), lax.axis_index("cfg")
     core, hi, z, x = lax.rem(win, 2), lax.rem(win // 2, 2), lax.rem(win // 4, 4), win // 16
@@ -68,9 +68,6 @@
         first[c, 3, 0:24, :] = wo_ref[:, 384 * c:384 * (c + 1)]
         for i in range(4):
             first[c, i, 24:32, :] = jnp.zeros((8, 384), BF16)
-    edge[:, 64:128] = jnp.zeros((32, 64), F32)
-    edge[0:16, 0:64] = lat_ref[0:16]
-    edge[16:32, 0:64] = lat_ref[496:512]
     pl.semaphore_wait(barrier, len(partners))
 
     mine = hi * 2 + core
@@ -83,8 +80,8 @@
     go(remote(first.at[1 - core], arrived0.at[mine], s0.at[0], r0.at[mine], sibling))
     for c in range(2):
         go(remote(first.at[c], arrived0.at[mine], s0.at[1 + c], r0.at[mine], across[c]))
-    go(remote(edge.at[0:16], lat_out.at[1], ls.at[0], lr.at[1], (left, cfg)))
-    go(remote(edge.at[16:32], lat_out.at[0], ls.at[1], lr.at[0], (right, cfg)))
+    go(remote(lat_ref.at[:, 0:128], lat_out.at[1], ls.at[0], lr.at[1], (left, cfg)))
+    go(remote(lat_ref.at[:, 384:512], lat_out.at[0], ls.at[1], lr.at[0], (right, cfg)))
 
     def views(i):
         a1 = lambda p: wbuf.at[i, core, p, z, 0:48]
@@ -154,12 +151,14 @@
         rows = jnp.concatenate([arrived0[p, i].astype(F32)[0:24] for p in range(4)], axis=0)
         wbuf[i, core, x, z] = rows.astype(BF16)
 
+    gain = gain_ref[...][None, :]
+
     def norm_rows(b, carry):
         r = pl.ds(pl.multiple_of(b * 128, 128), 128)
         v = hid[r, :].astype(F32)
         centred = v - jnp.mean(v, axis=-1, keepdims=True)
         spread = jnp.mean(centred * centred, axis=-1, keepdims=True)
-        normed[r, :] = (centred * lax.rsqrt(spread + norm_eps) * gain_ref[...]).astype(BF16)
+        normed[r, :] = (centred * lax.rsqrt(spread + norm_eps) * gain).astype(BF16)
         return carry
 
     def turn_rows(b, carry):
@@ -167,8 +166,8 @@
         urel[:, r, :] = jnp.swapaxes(uin[r], 0, 1)
         return carry
 
-    hid_copy.wait()
-    lax.fori_loop(0, 4, norm_rows, 0)
+    uin_copy.wait()
+    lax.fori_loop(0, 8, turn_rows, 0)
     arrived0[mine] = first[core]
     for p in (hi * 2 + 1 - core, (1 - hi) * 2, (1 - hi) * 2 + 1):
         await_in(arrived0.at[p], s0.at[0], r0.at[p])
@@ -176,27 +175,43 @@
     launch(stage1(0))
     for i in range(1, CHUNKS):
         assemble(i)
-    lax.fori_loop(4, 8, norm_rows, 0)
+        launch(stage1(i))
+    for k in range(4):
+        go(remote(urel.at[k], u_oth.at[k, core], us.at[k], ur.at[k], facing))
+        go(remote(urel.at[4 + k], u_oth.at[4 + k, core], us.at[4 + k], ur.at[4 + k], opposite))
+    up_local = pltpu.make_async_copy(urel, u_own.at[:, core], load_sem.at[2])
+    up_local.start()
+    hid_copy.wait()
     stage1_in(0)
     launch(forward1(0))
-    pred[...] = jnp.dot(hid[...], proj_ref[...], preferred_element_type=F32)
+    lax.fori_loop(0, 4, norm_rows, 0)
+    for i in range(1, CHUNKS):
+        stage1_in(i)
+        launch(forward1(i))
     forward1_in(0)
     launch(stage2(0))
-    launch(stage1(1))
-    uin_copy.wait()
-    lax.fori_loop(0, 4, turn_rows, 0)
+    forward1_in(1)
+    launch(stage2(1))
+    lax.fori_loop(4, 8, norm_rows, 0)
+    forward1_in(2)
+    forward1_in(3)
     stage2_in(0)
     launch(forward2(0))
-    lax.fori_loop(4, 8, turn_rows, 0)
-
-    up_local = pltpu.make_async_copy(urel, u_own.at[:, core], load_sem.at[2])
-    up_local.start()
-    go(remote(urel, u_own.at[:, core], us.at[0], ur.at[0], sibling))
-    go(remote(urel.at[0:4], u_oth.at[0:4, core], us.at[1], ur.at[1], facing))
-    go(remote(urel.at[4:8], u_oth.at[4:8, core], us.at[2], ur.at[2], opposite))
+    launch(stage2(2))
+    pred[...] = lax.dot_general(hid[...], proj_ref[...], (((1,), (1,)), ((), ())), preferred_element_type=F32)
     forward2_in(0)
     launch(share(0))
+    stage2_in(1)
+    launch(forward2(1))
+    launch(stage2(3))
     share_in(0)
+    go(remote(urel, u_own.at[:, core], us.at[8], ur.at[8], sibling))
+
+    def pass_on(k):
+        for q in (k, k + 4):
+            piece = u_oth.at[q, core]
+            await_in(piece, us.at[q], ur.at[q])
+            remote(piece, piece, us.at[9 + q], ur.at[9 + q], sibling).start()
 
     lane_first = lax.broadcasted_iota(jnp.int32, (1, 128), 1) < 64
     one = jnp.ones((), BF16)
@@ -204,8 +219,6 @@
 
     def chunk(i, carry):
         nxt = i + 1
-        stage1_in(nxt)
-        launch(forward1(nxt))
 
         def project(b, carry):
             r = pl.ds(pl.multiple_of(b * 256, 256), 256)
@@ -215,12 +228,13 @@
                 qkv[g, r, :] = res[:, g * 128:(g + 1) * 128]
             return carry
         lax.fori_loop(0, 4, project, 0)
-        forward1_in(nxt)
-        launch(stage2(nxt))
-
-        @pl.when(i < 2)
+        forward2_in(nxt)
+        launch(share(nxt))
+
+        @pl.when(i == 0)
         def _():
-            launch(stage1(nxt + 1))
+            stage2_in(2)
+            launch(forward2(2))
 
         def heads(c, carry):
             k, v = qkv[3 * c + 1], qkv[3 * c + 2]
@@ -239,21 +253,20 @@
                     attended[2 * i + c, t // 2 * 256:(t // 2 + 1) * 256] = jnp.where(lane_first, keep, o).astype(BF16)
                 keep, s = o, s_next
 
-            @pl.when(c == 0)
+            @pl.when((i == 0) & (c == 0))
             def _():
-                stage2_in(nxt)
-                launch(forward2(nxt))
+                stage2_in(3)
+                launch(forward2(3))
             return carry
         lax.fori_loop(0, 2, heads, 0)
-        forward2_in(nxt)
-        launch(share(nxt))
         share_in(nxt)
+        pass_on(i)
         return carry
     lax.fori_loop(0, 3, chunk, 0)
 
     factor = jnp.where(cfg == 0, guide_scale, 1.0 - guide_scale).astype(F32)
     wo = jnp.concatenate([wbuf[3, 0].reshape(1536, 384), wbuf[3, 1].reshape(1536, 384)], axis=1)
-    folded = lax.dot_general(proj_ref[...], wo, (((0,), (0,)), ((), ())), preferred_element_type=F32).astype(BF16)
+    folded = jnp.dot(proj_ref[...], wo, preferred_element_type=F32).astype(BF16)
     att = jnp.concatenate([attended[g] for g in range(6)], axis=1)
     total = pred[...] + lax.dot_general(att, folded, (((1,), (1,)), ((), ())), preferred_element_type=F32)
     xs[:, 0:64] = (factor * total).astype(BF16)
@@ -266,20 +279,19 @@
         go(remote(xs.at[1008:1024], pp_out.at[cfg], xsend.at[4 + c], xrecv.at[4 + cfg], (right2, to)))
     go(remote(xs.at[0:528], part_out, xsend.at[6], xrecv.at[6], facing))
 
-    await_in(u_oth.at[0:4, core], us.at[1], ur.at[1])
-    go(remote(u_oth.at[0:4, core], u_oth.at[0:4, core], us.at[3], ur.at[3], sibling))
-    await_in(u_oth.at[4:8, core], us.at[2], ur.at[2])
-    go(remote(u_oth.at[4:8, core], u_oth.at[4:8, core], us.at[4], ur.at[4], sibling))
-
+    pass_on(3)
     for c in range(2):
         await_in(prev_out.at[c], xsend.at[0], xrecv.at[c])
         await_in(nxt_out.at[c], xsend.at[0], xrecv.at[2 + c])
         await_in(pp_out.at[c], xsend.at[0], xrecv.at[4 + c])
         await_in(lat_out.at[c], ls.at[0], lr.at[c])
     await_in(part_out, xsend.at[6], xrecv.at[6])
-    await_in(u_own.at[:, 1 - core], us.at[0], ur.at[0])
-    await_in(u_oth.at[0:4, 1 - core], us.at[3], ur.at[3])
-    await_in(u_oth.at[4:8, 1 - core], us.at[4], ur.at[4])
+    await_in(u_own.at[:, 1 - core], us.at[8], ur.at[8])
+    for q in range(8):
+        theirs = u_oth.at[q, 1 - core]
+        await_in(theirs, us.at[9 + q], ur.at[9 + q])
+        piece = u_oth.at[q, core]
+        remote(piece, piece, us.at[9 + q], ur.at[9 + q], sibling).wait_send()
     up_local.wait()
     own_copy.wait()
     for copy in sends:
@@ -301,7 +313,7 @@
     return pl.pallas_call(
         front_kernel,
         out_shape=(shape((528, 128), BF16), shape((528, 128), BF16), shape((2, 528, 128), BF16),
-                   shape((2, 16, 128), BF16), shape((2, 16, 128), BF16), shape((2, 16, 128), F32),
+                   shape((2, 16, 128), BF16), shape((2, 16, 128), BF16), shape((2, 64, 128), F32),
                    shape((8, 2, 1024, 256), BF16), shape((8, 2, 1024, 256), BF16)),
         in_specs=[hbm, vm, vm, vm, vm, vm, hbm],
         out_specs=(hbm,) * 8,
@@ -315,11 +327,10 @@
             pltpu.VMEM((6, 1024, 128), BF16),
             pltpu.VMEM((1024, 64), F32),
             pltpu.VMEM((1024, 128), BF16),
-            pltpu.VMEM((32, 128), F32),
             pltpu.VMEM((1024, 8, 256), BF16),
             pltpu.VMEM((8, 1024, 256), BF16),
             dma((3,)), dma((3,)), dma((4,)), dma((CHUNKS, 15)), dma((CHUNKS, 15)),
-            dma((2,)), dma((2,)), dma((5,)), dma((5,)), dma((7,)), dma((7,)), dma,
+            dma((2,)), dma((2,)), dma((17,)), dma((17,)), dma((7,)), dma((7,)), dma,
         ],
         compiler_params=pltpu.CompilerParams(collective_id=0, has_side_effects=True,
                                              vmem_limit_bytes=56 * 1024 * 1024),
@@ -370,9 +381,9 @@
     row = jnp.where(row < 0, row + 512, jnp.where(row >= 512, row - 512, row))
     rising = (row.astype(F32) + 0.5) * (1.0 / 512)
     blended = rising * head + (1.0 - rising) * tail
-    extended = jnp.concatenate([halo_ref[0][:, :64], lat_ref[...], halo_ref[1][:, :64]], axis=0)
+    extended = jnp.concatenate([halo_ref[0].T[112:], lat_ref[...].T, halo_ref[1].T[:16]], axis=0)
     nxt_lat = extended + euler_step * blended[:, :64]
-    lat_out[...] = nxt_lat[16:528]
+    lat_out[...] = nxt_lat[16:528].T
     ext[0:544, :] = nxt_lat.astype(BF16).astype(F32)
     ext[544:560, :] = jnp.zeros((16, 64), F32)
 
@@ -428,7 +439,7 @@
     anyspec = pl.BlockSpec(memory_space=pl.ANY)
     return pl.pallas_call(
         decode_kernel,
-        out_shape=(jax.ShapeDtypeStruct((512, 64), F32), jax.ShapeDtypeStruct((2048, 512), BF16)),
+        out_shape=(jax.ShapeDtypeStruct((64, 512), F32), jax.ShapeDtypeStruct((2048, 512), BF16)),
         in_specs=[vm] * 11 + [anyspec] * 4,
         out_specs=(vm, vm),
         scratch_shapes=[
@@ -452,10 +463,11 @@
 def per_device(hidden, ln_gain, qkv_weight, out_weight, proj_weight, latent, conv_in_weight, snake_in,
                up_weight, snake_mid, res_weight, snake_out, mix_weight):
     own, part, prev, nxt, pp, halo, u_own, u_oth = front(
-        hidden[0], ln_gain.reshape(1, -1), qkv_weight, out_weight, proj_weight, latent, up_weight)
-    return decode_call(own, part, prev, nxt, pp, halo, latent, conv_in_weight,
+        hidden[0], ln_gain, qkv_weight, out_weight, proj_weight.T, latent.T, up_weight)
+    latent_next, decoded = decode_call(own, part, prev, nxt, pp, halo, latent.T, conv_in_weight,
                        snake_in.reshape(1, -1), snake_mid.reshape(1, -1), snake_out.reshape(1, -1),
                        u_own.reshape(8, 2048, 256), u_oth.reshape(8, 2048, 256), res_weight, mix_weight)
+    return latent_next.T, decoded
 
 
 def solution(mesh):

time: 132 us -> 108 us (0.82)
  Pallas kernels: 125 us -> 107 us
  local copies, waits for them, and re-layouts: 6.6 us -> 0 us
    pallas_call x1, Pallas kernels: 92.5 us -> 74.6 us  [front(): pl.pallas_call(front_kernel, out_shape=(shape((528, 128), BF16), shape((5...]
    unnamed x2 -> x0, local copies, waits for them, and re-layouts: 3.59 us -> none
    pallas_call x1 -> x0, local copies, waits for them, and re-layouts: 1.72 us -> none  [decode_call(): pl.pallas_call(decode_kernel, out_shape=(jax.ShapeDtypeStruct((512, 64),...]
where the time goes in v2:
time: 108 us
  Pallas kernels  107 us (99%)
    pallas_call x1, Pallas kernels, front(): pl.pallas_call(front_kernel, out_shape=(shape((528, 128), BF16), shape((5...  74.6 us
    pallas_call x1, Pallas kernels, decode_call(): pl.pallas_call(decode_kernel, out_shape=(jax.ShapeDtypeStruct((64, 512),...  32.2 us

profile of v2, /device:TPU:1, one launch (start us, length us, event | category | flops | bytes accessed | tf_op | source)
XLA Modules:
  0.0 107.6 jit_solution(1883322685615158469)
XLA Ops:
  0.6 74.6 %front.1 = (bf16[528,128]{1,0:T(8,128)(2,1)}, bf16[528,128]{1,0:T(8,128)(2,1)}, bf16[2,528,128]{2,1,0:T(8,128)(2,1)}, bf16[2,16,128]{2,1,0:T(8,128)(2,1)}, bf16[...) custom-call(bf16[1024,1536]{1,0:T(8,128)(2,1)} %bitcast.16, ...), custom_call_target="tpu_custom_call" | custom-call | flops 14000000000 | bytes 40000000 | tf_op jit(solution)/shard_map/front/pallas_call | solution.py:313
  75.3 32.2 %decode.1 = (f32[64,512]{1,0:T(8,128)}, bf16[2048,512]{1,0:T(8,128)(2,1)}) custom-call(bf16[528,128]{1,0:T(8,128)(2,1)} %get-tuple-element.12.own_ref, bf16[528,128]{1,0:T(8,128)(2,1)} %get-tuple-element.13.part_ref, bf16[2,528,128]{2,1,0:T(8,128)(2,1)} %get-tuple-element.14.prev_ref, bf16[2,16,128]{2,1,0:T(8,128)(2,1)} %get-tuple-element.15.nxt_ref, ...), custom_call_target="tpu_custom_call" | custom-call | tf_op jit(solution)/shard_map/decode/pallas_call | solution.py:440

commit v3 on v2

--- a/solution.py
+++ b/solution.py
@@ -220,14 +220,10 @@
     def chunk(i, carry):
         nxt = i + 1
 
-        def project(b, carry):
-            r = pl.ds(pl.multiple_of(b * 256, 256), 256)
-            w = jnp.concatenate([wbuf[i, 0].reshape(1536, 384), wbuf[i, 1].reshape(1536, 384)], axis=1)
-            res = jnp.dot(normed[r, :], w, preferred_element_type=F32).astype(BF16)
-            for g in range(6):
-                qkv[g, r, :] = res[:, g * 128:(g + 1) * 128]
-            return carry
-        lax.fori_loop(0, 4, project, 0)
+        w = jnp.concatenate([wbuf[i, 0].reshape(1536, 384), wbuf[i, 1].reshape(1536, 384)], axis=1)
+        res = jnp.dot(normed[...], w, preferred_element_type=F32).astype(BF16)
+        for g in range(6):
+            qkv[g] = res[:, g * 128:(g + 1) * 128]
         forward2_in(nxt)
         launch(share(nxt))
 
@@ -354,7 +350,7 @@
 
 def decode_kernel(own_ref, part_ref, prev_ref, nxt_ref, pp_ref, halo_ref, lat_ref, cw_ref, a_in_ref, a_mid_ref, a_out_ref,
                   u_own, u_oth, res_hbm, mix_hbm, lat_out, dec_out,
-                  ext, lifted, pair, ubuf, act, ups, res, mix, outf, u_sem, w_sem):
+                  ext, lifted, pair, ubuf, turned, act, ups, res, mix, outf, u_sem, w_sem):
     side = lax.axis_index("cfg")
     ucopies = []
     for j in range(8):
@@ -362,10 +358,13 @@
             cp = pltpu.make_async_copy(src.at[j], ubuf.at[j, h], u_sem.at[j, h])
             cp.start()
             ucopies.append(cp)
-    rcopy = pltpu.make_async_copy(res_hbm, res, w_sem.at[0])
-    rcopy.start()
-    mcopy = pltpu.make_async_copy(mix_hbm, mix, w_sem.at[1])
-    mcopy.start()
+    halves = [pl.ds(pl.multiple_of(first * 256, 256), 256) for first in (side, 1 - side)]
+    wcopies = []
+    for h in range(2):
+        wcopies.append(pltpu.make_async_copy(res_hbm.at[:, halves[h]], res.at[:, 256 * h:256 * h + 256], w_sem.at[h]))
+        wcopies.append(pltpu.make_async_copy(mix_hbm.at[:, halves[h]], mix.at[:, 256 * h:256 * h + 256], w_sem.at[2 + h]))
+    for copy in wcopies:
+        copy.start()
 
     def f32(x):
         return x.astype(F32)
@@ -397,41 +396,61 @@
     pair[:, 0:1024] = lifted[1:265, :].astype(BF16)
     pair[:, 1024:2048] = lifted[0:264, :].astype(BF16)
 
-    a_mid = a_mid_ref[...]
+    a_mid = jnp.concatenate([a_mid_ref[:, halves[0]], a_mid_ref[:, halves[1]]], axis=1)
     mid_scale, mid_inv = a_mid * (1 / math.pi), 1.0 / a_mid
     lhs = pair[...]
 
-    for j in range(8):
-        for h in range(2):
-            ucopies[2 * j + h].wait()
-            cols = pl.multiple_of((side * (1 - 2 * h) + h) * 256, 256)
-            outf_blk = jnp.dot(lhs, ubuf[j, h], preferred_element_type=F32)
-            lifted[0:264, pl.ds(cols, 256)] = outf_blk
-        blk = lifted[0:264, 0:512]
-        s = snake(blk, mid_scale, mid_inv)
-        if j < 4:
-            ups[j + 4] = lifted[1:257, 0:512]
-        else:
-            ups[j - 4] = blk[0:256]
-        act[j] = s[0:256].astype(BF16)
-        lifted[0:264, 512:1024] = s
-        act[j + 8] = lifted[1:257, 512:1024].astype(BF16)
-
-    rcopy.wait()
-    mcopy.wait()
+    def raise_two(g):
+        for q in range(4):
+            ucopies[4 * g + q].wait()
+        w = jnp.concatenate([ubuf[2 * g, 0], ubuf[2 * g, 1], ubuf[2 * g + 1, 0], ubuf[2 * g + 1, 1]], axis=1)
+        return jnp.dot(lhs, w, preferred_element_type=F32)
+
+    def keep_two(g, both):
+        for q in range(2):
+            j = 2 * g + q
+            blk = both[:, 512 * q:512 * q + 512]
+            s = snake(blk, mid_scale, mid_inv)
+            act[j] = s[0:256].astype(BF16)
+            turned[2 * q + 1] = s
+            act[j + 8] = turned[2 * q + 1, 1:257, :].astype(BF16)
+            if j < 4:
+                turned[2 * q] = blk
+                ups[j + 4] = turned[2 * q, 1:257, :]
+            else:
+                ups[j - 4] = blk[0:256]
+
+    both = raise_two(0)
+    for g in range(4):
+        later = raise_two(g + 1) if g < 3 else None
+        keep_two(g, both)
+        both = later
+
+    for copy in wcopies:
+        copy.wait()
     a_out = a_out_ref[...]
     out_scale, out_inv = a_out * (1 / math.pi), 1.0 / a_out
 
-    def step(i, carry):
+    def convolve(i):
         conv = None
         for k in range(7):
-            d = jnp.dot(act[i + 1 + k], res[k], preferred_element_type=F32)
+            d = jnp.dot(act[2 * i + 1 + k:2 * i + 3 + k].reshape(512, 512), res[k], preferred_element_type=F32)
             conv = d if conv is None else conv + d
+        return conv
+
+    def finish(i, conv):
         second = snake(conv, out_scale, out_inv).astype(BF16)
-        outf[:, i, :] = ups[i] + jnp.dot(second, mix[...], preferred_element_type=F32)
-        return carry
-    lax.fori_loop(0, 8, step, 0)
-    dec_out[...] = outf[...].reshape(2048, 512).astype(BF16)
+        mixed = jnp.dot(second, mix[...], preferred_element_type=F32)
+        for q in range(2):
+            outf[:, 2 * i + q, :] = ups[2 * i + q] + mixed[256 * q:256 * q + 256]
+
+    conv = convolve(0)
+    for i in range(4):
+        later = convolve(i + 1) if i < 3 else None
+        finish(i, conv)
+        conv = later
+    for h in range(2):
+        dec_out[:, halves[h]] = outf[:, :, 256 * h:256 * h + 256].reshape(2048, 256).astype(BF16)
 
 
 def decode_call(own, part, prev, nxt, pp, halo, lat, cw, a_in, a_mid, a_out, u_own, u_oth, res, mix):
@@ -447,13 +466,14 @@
             pltpu.VMEM((272, 1024), F32),
             pltpu.VMEM((264, 2048), BF16),
             pltpu.VMEM((8, 2, 2048, 256), BF16),
+            pltpu.VMEM((4, 264, 512), F32),
             pltpu.VMEM((16, 256, 512), BF16),
             pltpu.VMEM((8, 256, 512), F32),
             pltpu.VMEM((7, 512, 512), BF16),
             pltpu.VMEM((512, 512), BF16),
             pltpu.VMEM((256, 8, 512), F32),
             pltpu.SemaphoreType.DMA((8, 2)),
-            pltpu.SemaphoreType.DMA((2,)),
+            pltpu.SemaphoreType.DMA((4,)),
         ],
         compiler_params=pltpu.CompilerParams(vmem_limit_bytes=56 * 1024 * 1024),
         name="decode",

time: 108 us -> 97.8 us (0.906)
  Pallas kernels: 107 us -> 96.8 us
    pallas_call x1, Pallas kernels: 32.2 us -> 23.2 us  [decode_call(): pl.pallas_call(decode_kernel, out_shape=(jax.ShapeDtypeStruct((64, 512),...]
where the time goes in v3:
time: 97.8 us; the launch traced here: 97.6 us
  Pallas kernels  96.8 us (99%)
    pallas_call x1, Pallas kernels, front(): pl.pallas_call(front_kernel, out_shape=(shape((528, 128), BF16), shape((5...  73.6 us
    pallas_call x1, Pallas kernels, decode_call(): pl.pallas_call(decode_kernel, out_shape=(jax.ShapeDtypeStruct((64, 512),...  23.2 us

profile of v3, /device:TPU:1, one launch (start us, length us, event | category | flops | bytes accessed | tf_op | source)
XLA Modules:
  0.0 97.6 jit_solution(15377628788522215819)
XLA Ops:
  0.6 73.6 %front.1 = (bf16[528,128]{1,0:T(8,128)(2,1)}, bf16[528,128]{1,0:T(8,128)(2,1)}, bf16[2,528,128]{2,1,0:T(8,128)(2,1)}, bf16[2,16,128]{2,1,0:T(8,128)(2,1)}, bf16[...) custom-call(bf16[1024,1536]{1,0:T(8,128)(2,1)} %bitcast.16, ...), custom_call_target="tpu_custom_call" | custom-call | flops 14000000000 | bytes 40000000 | tf_op jit(solution)/shard_map/front/pallas_call | solution.py:309
  74.2 23.2 %decode.1 = (f32[64,512]{1,0:T(8,128)}, bf16[2048,512]{1,0:T(8,128)(2,1)}) custom-call(bf16[528,128]{1,0:T(8,128)(2,1)} %get-tuple-element.12.own_ref, bf16[528,128]{1,0:T(8,128)(2,1)} %get-tuple-element.13.part_ref, bf16[2,528,128]{2,1,0:T(8,128)(2,1)} %get-tuple-element.14.prev_ref, bf16[2,16,128]{2,1,0:T(8,128)(2,1)} %get-tuple-element.15.nxt_ref, ...), custom_call_target="tpu_custom_call" | custom-call | tf_op jit(solution)/shard_map/decode/pallas_call | solution.py:459

commit v4 on v3

--- a/solution.py
+++ b/solution.py
@@ -137,11 +137,25 @@
             await_in(two(far, 0, 2), gs.at[i, k + 5], gr.at[i, k + 5])
             await_in(two(far, 2, 2), gs.at[i, k + 6], gr.at[i, k + 6])
 
-    def share(i):
-        return [remote(wbuf.at[i, core], wbuf.at[i, core], gs.at[i, 14], gr.at[i, 14], sibling)]
+    def part(i, carrier, v, r):
+        return wbuf.at[i, carrier, pl.ds(0, 4), r, 0:48] if v == 0 else wbuf.at[i, carrier, r, pl.ds(0, 4), 48:96]
+
+    def slots(v):
+        return (z, z_up, z_dn, lax.rem(z + 2, 4)) if v == 0 else (x, x_up, x_dn, lax.rem(x + 2, 4))
+
+    def share(i, lo, hi):
+        out = []
+        for v in range(2):
+            for n, r in enumerate(slots(v)[lo:hi], lo):
+                k = 14 + 4 * v + n
+                out.append(remote(part(i, core, v, r), part(i, core, v, r), gs.at[i, k], gr.at[i, k], sibling))
+        return out
 
     def share_in(i):
-        await_in(wbuf.at[i, 1 - core], gs.at[i, 14], gr.at[i, 14])
+        for v in range(2):
+            for n, r in enumerate(slots(v)):
+                k = 14 + 4 * v + n
+                await_in(part(i, 1 - core, v, r), gs.at[i, k], gr.at[i, k])
 
     def launch(copies):
         for copy in copies:
@@ -198,9 +212,10 @@
     stage2_in(0)
     launch(forward2(0))
     launch(stage2(2))
+    launch(share(0, 0, 3))
     pred[...] = lax.dot_general(hid[...], proj_ref[...], (((1,), (1,)), ((), ())), preferred_element_type=F32)
     forward2_in(0)
-    launch(share(0))
+    launch(share(0, 3, 4))
     stage2_in(1)
     launch(forward2(1))
     launch(stage2(3))
@@ -225,7 +240,7 @@
         for g in range(6):
             qkv[g] = res[:, g * 128:(g + 1) * 128]
         forward2_in(nxt)
-        launch(share(nxt))
+        launch(share(nxt, 0, 4))
 
         @pl.when(i == 0)
         def _():
@@ -294,7 +309,7 @@
         copy.wait_send()
 
     def drain(i, carry):
-        for copies in (stage1(i), forward1(i), stage2(i), forward2(i), share(i)):
+        for copies in (stage1(i), forward1(i), stage2(i), forward2(i), share(i, 0, 4)):
             for copy in copies:
                 copy.wait_send()
         return carry
@@ -325,7 +340,7 @@
             pltpu.VMEM((1024, 128), BF16),
             pltpu.VMEM((1024, 8, 256), BF16),
             pltpu.VMEM((8, 1024, 256), BF16),
-            dma((3,)), dma((3,)), dma((4,)), dma((CHUNKS, 15)), dma((CHUNKS, 15)),
+            dma((3,)), dma((3,)), dma((4,)), dma((CHUNKS, 22)), dma((CHUNKS, 22)),
             dma((2,)), dma((2,)), dma((17,)), dma((17,)), dma((7,)), dma((7,)), dma,
         ],
         compiler_params=pltpu.CompilerParams(collective_id=0, has_side_effects=True,

time: 97.8 us -> 97.4 us (level)
  no operation moved by 1% of the time
where the time goes in v4:
time: 97.4 us; the launch traced here: 97.3 us
  Pallas kernels  96.5 us (99%)
    pallas_call x1, Pallas kernels, front(): pl.pallas_call(front_kernel, out_shape=(shape((528, 128), BF16), shape((5...  73.2 us
    pallas_call x1, Pallas kernels, decode_call(): pl.pallas_call(decode_kernel, out_shape=(jax.ShapeDtypeStruct((64, 512),...  23.2 us

profile of v4, /device:TPU:1, one launch (start us, length us, event | category | flops | bytes accessed | tf_op | source)
XLA Modules:
  0.0 97.3 jit_solution(12163025454997939584)
XLA Ops:
  0.6 73.2 %front.1 = (bf16[528,128]{1,0:T(8,128)(2,1)}, bf16[528,128]{1,0:T(8,128)(2,1)}, bf16[2,528,128]{2,1,0:T(8,128)(2,1)}, bf16[2,16,128]{2,1,0:T(8,128)(2,1)}, bf16[...) custom-call(bf16[1024,1536]{1,0:T(8,128)(2,1)} %bitcast.16, ...), custom_call_target="tpu_custom_call" | custom-call | flops 14000000000 | bytes 40000000 | tf_op jit(solution)/shard_map/front/pallas_call | solution.py:324
  73.9 23.2 %decode.1 = (f32[64,512]{1,0:T(8,128)}, bf16[2048,512]{1,0:T(8,128)(2,1)}) custom-call(bf16[528,128]{1,0:T(8,128)(2,1)} %get-tuple-element.12.own_ref, bf16[528,128]{1,0:T(8,128)(2,1)} %get-tuple-element.13.part_ref, bf16[2,528,128]{2,1,0:T(8,128)(2,1)} %get-tuple-element.14.prev_ref, bf16[2,16,128]{2,1,0:T(8,128)(2,1)} %get-tuple-element.15.nxt_ref, ...), custom_call_target="tpu_custom_call" | custom-call | tf_op jit(solution)/shard_map/decode/pallas_call | solution.py:474
